TPU v7x, 512 devices: a whole 4x8x8 slice. The times are simulated.
512 devices in a mesh: dp: 32 (over x, y), tp: 16 (over z, core).
Axes of the slice: x: 4, y: 8, z: 8, core: 2. Of those that a mesh axis runs over, the one named last changes fastest.
Arguments:
- embeddings: bfloat16 [12288, 192, 256], P(('dp', 'tp')), may hold values from -6 to 6
- projection: bfloat16 [256, 16], replicated, may hold values from -0.375 to 0.375
- compress: bfloat16 [256, 4], replicated, may hold values from -0.375 to 0.375
- w_up: bfloat16 [4096, 4096], P(None, 'tp'), may hold values from -0.09375 to 0.09375
- w_down: bfloat16 [4096, 768], P('tp'), may hold values from -0.125 to 0.125
- output_norm_gain: float32 [1536], P('tp'), may hold values from 0.25 to 1.75
- out_grad: bfloat16 [12288, 1536], P('dp', 'tp'), may hold values from -6 to 6
Outputs:
- block_result: bfloat16 [12288, 1536], P('dp', 'tp')
- grad_down: float32 [4096, 768], P(('tp', 'dp'))
All inputs are finite; a program needn't handle non-finite values.
Results may differ from a plain program's by a relative error of at most 0.017.
Values may be sent and summed in bfloat16 or wider, within the bound.
No kernel may reach another device: no remote copies, remote signals or barrier semaphores. Data moves between devices by JAX's collectives and lax.ppermute only.
A program may use at most 64 MiB of HBM per device.

v0:
```python
import jax
import jax.numpy as jnp
from jax import lax
from jax.sharding import PartitionSpec as P


def split_up(x, dim, devices):
    before, after = (x.shape[:dim], x.shape[dim + 1 :])
    return jnp.moveaxis(x.reshape(*before, devices, -1, *after), dim, 0)


def summed_on_arrival(x, axis, dim):
    parts = split_up(x, dim, lax.axis_size(axis))
    arrived = lax.all_to_all(parts, axis, split_axis=0, concat_axis=0, tiled=True)
    return arrived.astype(jnp.float32).sum(axis=0)


def sent_to_all(x, axis):
    devices = lax.axis_size(axis)
    return lax.all_to_all(jnp.broadcast_to(x[None], (devices, *x.shape)), axis, 0, 0, tiled=True)


def gathered_once(x, axis):
    leaves = jax.tree.leaves(x)
    sequence = sorted(range(len(leaves)), key=lambda k: -leaves[k].size)
    width = (1, *leaves[sequence[0]].shape)[-1]
    lines = [
        jnp.pad(leaves[k].reshape(-1), (0, -leaves[k].size % width)).reshape(-1, width)
        for k in sequence
    ]
    both, at, found = (sent_to_all(jnp.concatenate(lines), axis), 0, {})
    for k, line in zip(sequence, lines):
        share = both[:, at : at + len(line)].reshape(len(both), -1)
        found[k] = share[:, : leaves[k].size].reshape(-1, *leaves[k].shape)
        at += len(line)
    numbers = iter(range(len(leaves)))
    return jax.tree.map(lambda _: found[next(numbers)], x)


def joined_by_halves(pieces, combine):
    while len(jax.tree.leaves(pieces)[0]) > 1:
        pieces = jax.vmap(combine)(
            *(jax.tree.map(lambda part: part[side::2], pieces) for side in (0, 1))
        )
    return jax.tree.map(lambda part: part[0], pieces)


def joined_all(x, axis, combine):
    pieces = gathered_once(x, axis)
    return joined_by_halves(pieces, combine)


def turned_gather(arrays, axis, dims):
    turned = [jnp.moveaxis(a, dim, 0) for a, dim in zip(arrays, dims)]
    both = jnp.concatenate([t.reshape(len(t), -1) for t in turned], axis=1)
    filled, at, done = (lax.all_gather(both, axis, axis=0, tiled=True), 0, [])
    for t, dim in zip(turned, dims):
        share = filled[:, at : at + t[0].size].reshape(-1, *t.shape[1:])
        done.append(jnp.moveaxis(share, 0, dim))
        at += t[0].size
    return tuple(done)


def chan_merge(left, right):
    count_a, mean_a, dev_a = left
    count_b, mean_b, dev_b = right
    total = count_a + count_b
    delta = mean_b - mean_a
    row_average = mean_a + delta * (count_b / total)
    dev = dev_a + dev_b + delta * delta * (count_a * count_b / total)
    return (total, row_average, dev)


def on_device(embeddings, projection, compress, w_up, w_down, output_norm_gain, out_grad):
    samples = embeddings.shape[0]
    pairs = jnp.einsum(
        "sef,fk->sek", embeddings, projection, preferred_element_type=jnp.float32
    ).astype(jnp.bfloat16)
    inter = jnp.einsum(
        "sek,sef->skf", pairs, embeddings, preferred_element_type=jnp.float32
    ).reshape(samples, -1)
    center = inter - jnp.mean(inter, axis=1, keepdims=True)
    spread = jnp.mean(center * center, axis=1, keepdims=True)
    normed = (center / jnp.sqrt(spread + 1e-05)).astype(jnp.bfloat16)
    lcb = jnp.einsum(
        "sef,fj->sje", embeddings, compress, preferred_element_type=jnp.float32
    ).reshape(samples, -1)
    hidden = jax.nn.gelu(
        jnp.dot(
            lax.all_gather(normed, "tp", axis=0, tiled=True),
            w_up,
            preferred_element_type=jnp.float32,
        ),
        approximate=True,
    ).astype(jnp.bfloat16)
    group_rows = hidden.shape[0]
    tp_count = lax.axis_size("tp")
    mlp = jnp.dot(hidden, w_down, preferred_element_type=jnp.float32)
    mlp_width = mlp.shape[1]
    full_width = mlp_width + lcb.shape[1]
    width = full_width // tp_count
    mlp_share = summed_on_arrival(mlp.astype(jnp.bfloat16), "tp", 1)
    lcb_share = lax.all_to_all(
        lcb.astype(jnp.bfloat16), "tp", split_axis=1, concat_axis=0, tiled=True
    ).astype(lcb.dtype)
    mixed_rows = jnp.concatenate([mlp_share, lcb_share], axis=1)
    own_mean = jnp.mean(mixed_rows, axis=1)
    own_dev = jnp.sum((mixed_rows - own_mean[:, None]) ** 2, axis=1)
    own_count = jnp.full((), width, jnp.float32)
    total, row_average, dev = joined_all((own_count, own_mean, own_dev), "tp", chan_merge)
    inverse_deviation = 1.0 / jnp.sqrt(dev[:, None] / total + 1e-05)
    centered_rows = (mixed_rows - row_average[:, None]) * inverse_deviation
    block_result = (centered_rows * output_norm_gain).astype(jnp.bfloat16)
    scaled_rows = out_grad.astype(jnp.float32) * output_norm_gain
    entire_scaled_rows, entire_normalized_rows = tuple(
        (
            part.astype(jnp.float32)
            for part in turned_gather(
                (scaled_rows.astype(jnp.bfloat16), centered_rows.astype(jnp.bfloat16)), "tp", (1, 1)
            )
        )
    )
    first_moment = jnp.mean(entire_scaled_rows, axis=1, keepdims=True)
    second_moment = jnp.mean(entire_scaled_rows * entire_normalized_rows, axis=1, keepdims=True)
    mixed_gradient = (
        (entire_scaled_rows - first_moment - entire_normalized_rows * second_moment)
        * inverse_deviation
    ).astype(jnp.bfloat16)
    group_mlp = mlp_width // tp_count
    mlp_grad = mixed_gradient.reshape(group_rows, tp_count, -1)[:, :, :group_mlp].reshape(
        group_rows, -1
    )
    grad_down = summed_on_arrival(
        jnp.einsum("rh,rc->hc", hidden, mlp_grad, preferred_element_type=jnp.float32).astype(
            jnp.bfloat16
        ),
        "dp",
        0,
    )
    return (block_result, grad_down)


def solution(mesh):
    return jax.shard_map(
        on_device,
        mesh=mesh,
        in_specs=(
            P(("dp", "tp"), None, None),
            P(),
            P(),
            P(None, "tp"),
            P("tp", None),
            P("tp"),
            P("dp", "tp"),
        ),
        out_specs=(P("dp", "tp"), P(("tp", "dp"), None)),
        check_vma=False,
    )
```

profile of v0, /device:TPU:8, one launch (start us, length us, event | category | flops | bytes accessed | tf_op | source)
XLA Modules:
  0.0 184.7 jit_solution(13328559922858504637)
XLA Ops:
  7.2 0.0 copy-start
  7.2 0.0 copy-start.3
  7.2 0.0 all-gather.3.cloned.1.call-start
  7.2 1.6 copy-done
  8.8 1.8 fusion.26
  10.7 0.4 multiply_reduce_fusion
  11.1 0.2 copy.26
  11.3 0.8 divide_convert_fusion
  12.1 0.0 all-gather.3.cloned.1.call-update
  12.1 0.0 copy-done.3
  12.1 0.7 fusion.6
  12.9 0.1 convert_element_type.74
  13.0 0.8 reshape.145
  13.8 10.4 %all-to-all-start.1 = ((bf16[16,2,576]{2,1,0:T(2,128)(2,1)}), bf16[16,2,576]{2,1,0:T(2,128)(2,1)S(1)}, u32[]{:S(2)}, u32[]{:S(2)}) async-start(bf16[16,2,576]{2,1,0:T(2,128)(2,1)} %reshape.145), calls=%async_computation.1 | async-start | bytes 81920 | tf_op jit(solution)/shard_map/all_to_all | solution.py:103
  24.2 37.1 %all-gather.3.cloned.1.call-done = bf16[384,4096]{1,0:T(8,128)(2,1)} async-done(((bf16[24,4096]{1,0:T(8,128)(2,1)}), bf16[384,4096]{1,0:T(8,128)(2,1)}) %all-gather.3.cloned.1.call-update) | async-done | bytes 3145744 | tf_op jit(solution)/shard_map/all_gather | solution.py:90
  61.3 0.0 copy-start.6
  61.3 3.6 %fusion.29 = f32[384,256]{1,0:T(8,128)S(1)} fusion(bf16[384,4096]{1,0:T(8,128)(2,1)} %all-gather.3.cloned.1.call-done, bf16[4096,256]{1,0:T(8,128)(2,1)} %param.10), kind=kOutput, calls=%fused_computation.71 | convolution fusion | flops 805306368 | bytes 5636096 | tf_op jit(solution)/shard_map/dot_general | solution.py:89
  64.9 0.0 copy-start.7
  64.9 0.7 copy-done.7
  65.7 0.0 copy-done.6
  65.7 0.4 convolution_convert_fusion
  66.0 0.0 copy-start.4
  66.1 0.0 copy-start.2
  66.1 0.0 copy-start.5
  66.1 1.0 copy.19
  67.1 0.0 all-to-all-done.1
  67.1 4.3 %all-to-all-start = ((bf16[16,384,48]{1,2,0:T(8,128)(2,1)}), bf16[16,384,48]{1,2,0:T(8,128)(2,1)S(1)}, u32[]{:S(2)}, u32[]{:S(2)}) async-start(bf16[16,384,48]{1,2,0:T(8,128)(2,1)} %bitcast.2), calls=%async_computation | async-start | bytes 1179648 | tf_op jit(solution)/shard_map/all_to_all | solution.py:14
  71.4 0.0 all-gather.5.cloned.1.call-start
  71.5 0.1 reshape.146
  71.6 0.1 convert_reduce_fusion.4
  71.8 0.1 reduce_sum.108
  71.9 0.1 reduce_sum.110
  72.0 0.1 copy.21
  72.1 16.6 %all-to-all-done = bf16[16,384,48]{1,2,0:T(8,128)(2,1)S(1)} async-done(((bf16[16,384,48]{1,2,0:T(8,128)(2,1)}), bf16[16,384,48]{1,2,0:T(8,128)(2,1)S(1)}, u32[]{:S(2)}, u32[]{:S(2)}) %all-to-all-start) | async-done | bytes 589856 | tf_op jit(solution)/shard_map/all_to_all | solution.py:14
  88.7 0.2 convert_reduce_fusion.1
  88.9 0.0 copy-done.4
  89.0 12.5 %all_to_all.25 = f32[16,3,384]{2,1,0:T(4,128)S(1)} all-to-all(f32[16,3,384]{2,1,0:T(4,128)S(1)} %broadcast_in_dim.2), channel_id=1, replica_groups=mesh['dp'=32,'tp'=16] {'tp'}, dimensions={0} | all-to-all | bytes 147456 | tf_op jit(solution)/shard_map/all_to_all | solution.py:20
  101.5 0.1 fusion.24
  101.7 0.1 slice_reduce_fusion
  101.8 0.1 slice.104
  101.9 0.1 slice.105
  102.0 0.1 slice.108
  102.1 0.1 slice.109
  102.2 0.1 slice.112
  102.3 0.1 slice.113
  102.4 0.6 fusion.25
  105.6 0.1 multiply_add_fusion
  105.8 0.1 multiply_add_fusion.2
  106.6 0.1 multiply_add_fusion.4
  106.8 0.0 copy-done.2
  106.8 0.0 copy-done.5
  106.8 0.7 fusion.16
  107.5 0.7 pad_maximum_fusion.1
  108.2 0.0 all-gather.5.cloned.1.call-update
  108.2 40.1 %all-gather.5.cloned.1.call-done = bf16[1536,768]{1,0:T(8,128)(2,1)} async-done(((bf16[96,768]{1,0:T(8,128)(2,1)}), bf16[1536,768]{1,0:T(8,128)(2,1)}) %all-gather.5.cloned.1.call-update) | async-done | bytes 2359312 | tf_op jit(solution)/shard_map/all_gather | solution.py:56
  148.3 0.0 copy-start.1
  148.3 2.2 %convert_reduce_fusion = (f32[384]{0:T(512)S(1)}, f32[384]{0:T(512)S(1)}) fusion(bf16[1536,768]{1,0:T(8,128)(2,1)} %all-gather.5.cloned.1.call-done), kind=kLoop, calls=%fused_computation.2 | loop fusion | flops 2948352 | bytes 2362368 | tf_op jit(solution)/shard_map/reduce_sum | solution.py:123
  150.6 0.1 copy-done.1
  150.7 0.5 fusion.2
  151.2 0.1 slice.140
  151.3 0.4 copy-done.8
  151.7 0.5 fusion.4
  152.2 25.1 %all_to_all.26 = bf16[32,8,768]{2,1,0:T(8,128)(2,1)S(1)} all-to-all(bf16[32,8,768]{2,1,0:T(8,128)(2,1)S(1)} %fusion.4), channel_id=1, replica_groups=mesh['dp'=32,'tp'=16] {'dp'}, dimensions={0} | all-to-all | bytes 786432 | tf_op jit(solution)/shard_map/all_to_all | solution.py:14
  177.2 0.7 convert_reduce_fusion.3
  (34 shorter events, 0.5 us)
Async XLA Ops:
  7.2 1.7 copy-start
  7.2 5.0 %copy-start.3 = (bf16[256,4]{0,1:T(4,128)(2,1)S(1)}, bf16[256,4]{0,1:T(4,128)(2,1)}, u32[]{:S(2)}) copy-start(bf16[256,4]{0,1:T(4,128)(2,1)} %param.9) | copy-start | bytes 6148
  7.2 54.2 %all-gather.3.cloned.1.call-start = ((), (), s32[]{:S(2)}) async-start(), calls=%async_computation.4 | async-start | bytes 3342336 | tf_op jit(solution)/shard_map/all_gather | solution.py:90
  13.8 53.3 %all-to-all-start.1 = ((bf16[16,2,576]{2,1,0:T(2,128)(2,1)}), bf16[16,2,576]{2,1,0:T(2,128)(2,1)S(1)}, u32[]{:S(2)}, u32[]{:S(2)}) async-start(bf16[16,2,576]{2,1,0:T(2,128)(2,1)} %reshape.145), calls=%async_computation.1 | async-start | bytes 81920 | tf_op jit(solution)/shard_map/all_to_all | solution.py:103
  61.3 4.3 %copy-start.6 = (bf16[256,768]{1,0:T(8,128)(2,1)S(1)}, bf16[256,768]{1,0:T(8,128)(2,1)}, u32[]{:S(2)}) copy-start(bf16[256,768]{1,0:T(8,128)(2,1)} %param.11) | copy-start | bytes 1179652
  64.9 0.7 copy-start.7
  66.0 22.9 %copy-start.4 = (f32[1,384]{1,0:T(1,128)S(1)}, f32[1,384]{1,0:T(1,128)}, u32[]{:S(2)}) copy-start(f32[1,384]{1,0:T(1,128)} %constant.29.clone.1) | copy-start | bytes 4612
  66.1 40.7 %copy-start.2 = (bf16[384,96]{0,1:T(8,128)(2,1)S(1)}, bf16[384,96]{0,1:T(8,128)(2,1)}, u32[]{:S(2)}) copy-start(bf16[384,96]{0,1:T(8,128)(2,1)} %param.13) | copy-start | bytes 221188
  66.1 40.7 %copy-start.5 = (f32[96]{0:T(128)S(1)}, f32[96]{0:T(128)}, u32[]{:S(2)}) copy-start(f32[96]{0:T(128)} %param.12) | copy-start | bytes 1156
  67.1 21.5 %all-to-all-start = ((bf16[16,384,48]{1,2,0:T(8,128)(2,1)}), bf16[16,384,48]{1,2,0:T(8,128)(2,1)S(1)}, u32[]{:S(2)}, u32[]{:S(2)}) async-start(bf16[16,384,48]{1,2,0:T(8,128)(2,1)} %bitcast.2), calls=%async_computation | async-start | bytes 1179648 | tf_op jit(solution)/shard_map/all_to_all | solution.py:14
  71.4 76.9 %all-gather.5.cloned.1.call-start = ((), (), s32[]{:S(2)}) async-start(), calls=%async_computation.5 | async-start | bytes 2506752 | tf_op jit(solution)/shard_map/all_gather | solution.py:56
  148.3 2.4 %copy-start.1 = (bf16[1536,768]{1,0:T(8,128)(2,1)S(1)}, bf16[1536,768]{1,0:T(8,128)(2,1)}, u32[]{:S(2)}) copy-start(bf16[1536,768]{1,0:T(8,128)(2,1)} %all-gather.5.cloned.1.call-done) | copy-start | bytes 7077892
  150.7 1.0 copy-start.8
Sparse Core Ops, SparseCore 0:
  12.3 49.0 all-gather.2
  108.3 39.9 all-gather.4
where the time goes:
time: 185 us
  waiting for transfers between devices  93.8 us (51%)
  blocking collectives  37.6 us (20%)
  between operations  17.6 us (10%)
  starting transfers between devices  14.8 us (8%)
  local copies, waits for them, and re-layouts  7.2 us (4%)
  matrix products  6.93 us (4%)
  other arithmetic  6.77 us (4%)
    all_gather x1, waiting for transfers between devices, turned_gather(): filled, at, done = (lax.all_gather(both, axis, axis=0, tiled=True), 0, [])  40.1 us
    all_gather x1, waiting for transfers between devices, on_device(): lax.all_gather(normed, 'tp', axis=0, tiled=True)  37.1 us
    all_to_all x1, blocking collectives, summed_on_arrival(): lax.all_to_all(parts, axis, split_axis=0, concat_axis=0, tiled=True)  25.1 us
    all_to_all x1, waiting for transfers between devices, summed_on_arrival(): lax.all_to_all(parts, axis, split_axis=0, concat_axis=0, tiled=True)  16.6 us
    all_to_all x1, blocking collectives, sent_to_all(): lax.all_to_all(jnp.broadcast_to(x[None], (devices, *x.shape)), axis, 0, 0...  12.5 us
    all_to_all x1, starting transfers between devices, on_device(): lax.all_to_all(lcb.astype(jnp.bfloat16), 'tp', split_axis=1, concat_axis=...  10.4 us
    all_to_all x1, starting transfers between devices, summed_on_arrival(): lax.all_to_all(parts, axis, split_axis=0, concat_axis=0, tiled=True)  4.3 us
    unnamed x22, local copies, waits for them, and re-layouts  4.06 us
  transfers between devices with their start and end apart: 4, of which 3 were waited for; matrix products, arithmetic and copies ran while one was open for 4% of the time, Pallas kernels for 0%

commit v1 on v0

--- a/solution.py
+++ b/solution.py
@@ -1,7 +1,23 @@
+import functools
 import jax
 import jax.numpy as jnp
 from jax import lax
 from jax.sharding import PartitionSpec as P
+
+
+def state_sheet_in(body, mesh_ax, pos_dim, ndim_at):
+    return jnp.concatenate(
+        lax.all_to_all(
+            jnp.stack(jnp.split(body, lax.axis_size(mesh_ax), axis=pos_dim), axis=0),
+            axis_name=mesh_ax,
+            split_axis=0,
+            concat_axis=0,
+        ),
+        axis=ndim_at,
+    )
+
+
+balance_the_task = functools.partial(state_sheet_in, mesh_ax="tp", pos_dim=1, ndim_at=0)
 
 
 def split_up(x, dim, devices):
@@ -100,9 +116,7 @@
     full_width = mlp_width + lcb.shape[1]
     width = full_width // tp_count
     mlp_share = summed_on_arrival(mlp.astype(jnp.bfloat16), "tp", 1)
-    lcb_share = lax.all_to_all(
-        lcb.astype(jnp.bfloat16), "tp", split_axis=1, concat_axis=0, tiled=True
-    ).astype(lcb.dtype)
+    lcb_share = balance_the_task(lcb.astype(jnp.bfloat16)).astype(lcb.dtype)
     mixed_rows = jnp.concatenate([mlp_share, lcb_share], axis=1)
     own_mean = jnp.mean(mixed_rows, axis=1)
     own_dev = jnp.sum((mixed_rows - own_mean[:, None]) ** 2, axis=1)

time: 185 us -> 185 us (level)
    unnamed x22 -> x37, local copies, waits for them, and re-layouts: 4.06 us -> 5.14 us
where the time goes in v1:
time: 185 us
  waiting for transfers between devices  92.7 us (50%)
  blocking collectives  37.6 us (20%)
  between operations  17.6 us (10%)
  starting transfers between devices  14.8 us (8%)
  local copies, waits for them, and re-layouts  8.32 us (4%)
  matrix products  6.93 us (4%)
  other arithmetic  6.74 us (4%)
    all_gather x1, waiting for transfers between devices, turned_gather(): filled, at, done = (lax.all_gather(both, axis, axis=0, tiled=True), 0, [])  40.1 us
    all_gather x1, waiting for transfers between devices, on_device(): lax.all_gather(normed, 'tp', axis=0, tiled=True)  36 us
    all_to_all x1, blocking collectives, summed_on_arrival(): lax.all_to_all(parts, axis, split_axis=0, concat_axis=0, tiled=True)  25.1 us
    all_to_all x1, waiting for transfers between devices, summed_on_arrival(): lax.all_to_all(parts, axis, split_axis=0, concat_axis=0, tiled=True)  16.6 us
    all_to_all x1, blocking collectives, sent_to_all(): lax.all_to_all(jnp.broadcast_to(x[None], (devices, *x.shape)), axis, 0, 0...  12.5 us
    all_to_all x1, starting transfers between devices, state_sheet_in(): lax.all_to_all(jnp.stack(jnp.split(body, lax.axis_size(mesh_ax), axis=pos...  10.4 us
    unnamed x37, local copies, waits for them, and re-layouts  5.14 us
    all_to_all x1, starting transfers between devices, summed_on_arrival(): lax.all_to_all(parts, axis, split_axis=0, concat_axis=0, tiled=True)  4.31 us
  transfers between devices with their start and end apart: 4, of which 3 were waited for; matrix products, arithmetic and copies ran while one was open for 4% of the time, Pallas kernels for 0%

profile of v1, /device:TPU:8, one launch (start us, length us, event | category | flops | bytes accessed | tf_op | source)
XLA Modules:
  0.0 184.7 jit_solution(10610225385956325599)
XLA Ops:
  7.2 0.0 all-gather.3.cloned.1.call-start
  7.2 1.6 copy-done
  8.8 1.8 fusion.26
  10.7 0.4 multiply_reduce_fusion
  11.1 0.2 copy.23
  11.3 0.8 divide_convert_fusion
  12.1 0.0 all-gather.3.cloned.1.call-update
  12.1 0.7 fusion.6
  12.9 0.1 convert_element_type.69
  13.0 0.1 constant_dynamic-update-slice_fusion.14
  13.1 0.1 constant_dynamic-update-slice_fusion.13
  13.2 0.1 constant_dynamic-update-slice_fusion.12
  13.2 0.1 constant_dynamic-update-slice_fusion.11
  13.3 0.1 constant_dynamic-update-slice_fusion.10
  13.4 0.1 constant_dynamic-update-slice_fusion.9
  13.5 0.1 constant_dynamic-update-slice_fusion.8
  13.6 0.1 constant_dynamic-update-slice_fusion.6
  13.6 0.1 constant_dynamic-update-slice_fusion.5
  13.7 0.1 constant_dynamic-update-slice_fusion.4
  13.8 0.1 constant_dynamic-update-slice_fusion.3
  13.9 0.1 constant_dynamic-update-slice_fusion.2
  14.0 0.1 constant_dynamic-update-slice_fusion.1
  14.1 0.1 constant_dynamic-update-slice_fusion
  14.1 0.8 reshape.142
  14.9 10.4 %all-to-all-start.1 = ((bf16[16,2,576]{2,1,0:T(2,128)(2,1)}), bf16[16,2,576]{2,1,0:T(2,128)(2,1)S(1)}, u32[]{:S(2)}, u32[]{:S(2)}) async-start(bf16[16,2,576]{2,1,0:T(2,128)(2,1)} %reshape.142), calls=%async_computation.1 | async-start | bytes 81920 | tf_op jit(solution)/shard_map/all_to_all | solution.py:10
  25.4 36.0 %all-gather.3.cloned.1.call-done = bf16[384,4096]{1,0:T(8,128)(2,1)} async-done(((bf16[24,4096]{1,0:T(8,128)(2,1)}), bf16[384,4096]{1,0:T(8,128)(2,1)}) %all-gather.3.cloned.1.call-update) | async-done | bytes 3145744 | tf_op jit(solution)/shard_map/all_gather | solution.py:106
  61.3 3.6 %fusion.29 = f32[384,256]{1,0:T(8,128)S(1)} fusion(bf16[384,4096]{1,0:T(8,128)(2,1)} %all-gather.3.cloned.1.call-done, bf16[4096,256]{1,0:T(8,128)(2,1)} %param.10), kind=kOutput, calls=%fused_computation.101 | convolution fusion | flops 805306368 | bytes 5636096 | tf_op jit(solution)/shard_map/dot_general | solution.py:105
  64.9 0.7 copy-done.7
  65.7 0.4 convolution_convert_fusion
  66.1 1.0 copy.17
  67.1 4.3 %all-to-all-start = ((bf16[16,384,48]{1,2,0:T(8,128)(2,1)}), bf16[16,384,48]{1,2,0:T(8,128)(2,1)S(1)}, u32[]{:S(2)}, u32[]{:S(2)}) async-start(bf16[16,384,48]{1,2,0:T(8,128)(2,1)} %bitcast.2), calls=%async_computation | async-start | bytes 1179648 | tf_op jit(solution)/shard_map/all_to_all | solution.py:30
  71.4 0.0 all-gather.5.cloned.1.call-start
  71.5 0.1 reshape.143
  71.6 0.1 convert_reduce_fusion.4
  71.8 0.1 reduce_sum.105
  71.9 0.1 reduce_sum.107
  71.9 0.1 copy.18
  72.0 16.6 %all-to-all-done = bf16[16,384,48]{1,2,0:T(8,128)(2,1)S(1)} async-done(((bf16[16,384,48]{1,2,0:T(8,128)(2,1)}), bf16[16,384,48]{1,2,0:T(8,128)(2,1)S(1)}, u32[]{:S(2)}, u32[]{:S(2)}) %all-to-all-start) | async-done | bytes 589856 | tf_op jit(solution)/shard_map/all_to_all | solution.py:30
  88.6 0.2 convert_reduce_fusion.1
  89.0 12.5 %all_to_all.20 = f32[16,3,384]{2,1,0:T(4,128)S(1)} all-to-all(f32[16,3,384]{2,1,0:T(4,128)S(1)} %broadcast_in_dim.2), channel_id=1, replica_groups=mesh['dp'=32,'tp'=16] {'tp'}, dimensions={0} | all-to-all | bytes 147456 | tf_op jit(solution)/shard_map/all_to_all | solution.py:36
  101.5 0.1 fusion.24
  101.6 0.1 slice_reduce_fusion
  101.8 0.1 slice.104
  101.9 0.1 slice.105
  102.0 0.1 slice.108
  102.1 0.1 slice.109
  102.2 0.1 slice.112
  102.3 0.1 slice.113
  102.4 0.6 fusion.25
  105.6 0.1 multiply_add_fusion
  105.8 0.1 multiply_add_fusion.2
  106.6 0.1 multiply_add_fusion.4
  106.8 0.7 fusion.16
  107.5 0.7 pad_maximum_fusion.1
  108.2 0.0 all-gather.5.cloned.1.call-update
  108.2 40.1 %all-gather.5.cloned.1.call-done = bf16[1536,768]{1,0:T(8,128)(2,1)} async-done(((bf16[96,768]{1,0:T(8,128)(2,1)}), bf16[1536,768]{1,0:T(8,128)(2,1)}) %all-gather.5.cloned.1.call-update) | async-done | bytes 2359312 | tf_op jit(solution)/shard_map/all_gather | solution.py:72
  148.3 2.2 %convert_reduce_fusion = (f32[384]{0:T(512)S(1)}, f32[384]{0:T(512)S(1)}) fusion(bf16[1536,768]{1,0:T(8,128)(2,1)} %all-gather.5.cloned.1.call-done), kind=kLoop, calls=%fused_computation.2 | loop fusion | flops 2948352 | bytes 2362368 | tf_op jit(solution)/shard_map/reduce_sum | solution.py:137
  150.6 0.1 copy-done.1
  150.7 0.5 fusion.2
  151.2 0.1 slice.140
  151.3 0.4 copy-done.8
  151.7 0.5 fusion.4
  152.2 25.1 %all_to_all.21 = bf16[32,8,768]{2,1,0:T(8,128)(2,1)S(1)} all-to-all(bf16[32,8,768]{2,1,0:T(8,128)(2,1)S(1)} %fusion.4), channel_id=1, replica_groups=mesh['dp'=32,'tp'=16] {'dp'}, dimensions={0} | all-to-all | bytes 786432 | tf_op jit(solution)/shard_map/all_to_all | solution.py:30
  177.2 0.7 convert_reduce_fusion.3
  (48 shorter events, 0.5 us)
Async XLA Ops:
  7.2 1.7 copy-start
  7.2 5.0 %copy-start.3 = (bf16[256,4]{0,1:T(4,128)(2,1)S(1)}, bf16[256,4]{0,1:T(4,128)(2,1)}, u32[]{:S(2)}) copy-start(bf16[256,4]{0,1:T(4,128)(2,1)} %param.9) | copy-start | bytes 6148
  7.2 54.2 %all-gather.3.cloned.1.call-start = ((), (), s32[]{:S(2)}) async-start(), calls=%async_computation.4 | async-start | bytes 3342336 | tf_op jit(solution)/shard_map/all_gather | solution.py:106
  14.9 52.2 %all-to-all-start.1 = ((bf16[16,2,576]{2,1,0:T(2,128)(2,1)}), bf16[16,2,576]{2,1,0:T(2,128)(2,1)S(1)}, u32[]{:S(2)}, u32[]{:S(2)}) async-start(bf16[16,2,576]{2,1,0:T(2,128)(2,1)} %reshape.142), calls=%async_computation.1 | async-start | bytes 81920 | tf_op jit(solution)/shard_map/all_to_all | solution.py:10
  61.3 4.3 %copy-start.6 = (bf16[256,768]{1,0:T(8,128)(2,1)S(1)}, bf16[256,768]{1,0:T(8,128)(2,1)}, u32[]{:S(2)}) copy-start(bf16[256,768]{1,0:T(8,128)(2,1)} %param.11) | copy-start | bytes 1179652
  64.9 0.7 copy-start.7
  65.7 23.3 %copy-start.4 = (f32[1,384]{1,0:T(1,128)S(1)}, f32[1,384]{1,0:T(1,128)}, u32[]{:S(2)}) copy-start(f32[1,384]{1,0:T(1,128)} %constant.29.clone.1) | copy-start | bytes 4612
  66.0 40.7 %copy-start.2 = (bf16[384,96]{0,1:T(8,128)(2,1)S(1)}, bf16[384,96]{0,1:T(8,128)(2,1)}, u32[]{:S(2)}) copy-start(bf16[384,96]{0,1:T(8,128)(2,1)} %param.13) | copy-start | bytes 221188
  66.1 40.7 %copy-start.5 = (f32[96]{0:T(128)S(1)}, f32[96]{0:T(128)}, u32[]{:S(2)}) copy-start(f32[96]{0:T(128)} %param.12) | copy-start | bytes 1156
  67.1 21.5 %all-to-all-start = ((bf16[16,384,48]{1,2,0:T(8,128)(2,1)}), bf16[16,384,48]{1,2,0:T(8,128)(2,1)S(1)}, u32[]{:S(2)}, u32[]{:S(2)}) async-start(bf16[16,384,48]{1,2,0:T(8,128)(2,1)} %bitcast.2), calls=%async_computation | async-start | bytes 1179648 | tf_op jit(solution)/shard_map/all_to_all | solution.py:30
  71.4 76.9 %all-gather.5.cloned.1.call-start = ((), (), s32[]{:S(2)}) async-start(), calls=%async_computation.5 | async-start | bytes 2506752 | tf_op jit(solution)/shard_map/all_gather | solution.py:72
  148.3 2.4 %copy-start.1 = (bf16[1536,768]{1,0:T(8,128)(2,1)S(1)}, bf16[1536,768]{1,0:T(8,128)(2,1)}, u32[]{:S(2)}) copy-start(bf16[1536,768]{1,0:T(8,128)(2,1)} %all-gather.5.cloned.1.call-done) | copy-start | bytes 7077892
  150.7 1.0 copy-start.8
Sparse Core Ops, SparseCore 0:
  12.3 49.0 all-gather.2
  108.3 39.9 all-gather.4
